TPU v7x, 32 devices: a whole 2x2x4 slice. The times are simulated.
32 devices in a mesh: row: 4 (over z), col: 4 (over x, core), rep: 2 (over y).
Axes of the slice: x: 2, y: 2, z: 4, core: 2. Of those that a mesh axis runs over, the one named last changes fastest.
Arguments:
- density_blocks: bfloat16 [4, 16, 128, 256], P('row', ('col', 'rep')), may hold values from -1 to 1
- density_columns: int32 [4, 16, 2], P('row', ('col', 'rep')), may hold values from 0 to 3, as said below
- square_pattern: int32 [4, 16, 2], P('row', ('col', 'rep')), may hold values from 0 to 3
- cube_pattern: int32 [4, 16, 2], P('row', ('col', 'rep')), may hold values from 0 to 3
Outputs:
- purified: float32 [4, 16, 128, 256], P('row', ('col', 'rep'))
Inputs may be any that keep to these rules, and one draw needn't show every extreme that they name: `density_columns`: the 2 block columns of one block row within one tile are all different.
All inputs are finite; a program needn't handle non-finite values.
Results may differ from a plain program's by a relative error of at most 0.0029.
Values may be sent and summed in bfloat16 or wider, within the bound.
A program may use at most 64 MiB of HBM per device.

v0:
```python
import jax
import jax.numpy as jnp
from jax import lax
from jax.sharding import PartitionSpec as P


def rows_times_column(left_blocks, left_cols, column_blocks, column_cols, targets):
    tile_count, row_count, block_size, left_width = left_blocks.shape
    left_slots = left_width // block_size
    tile_rows = column_blocks.shape[0] // tile_count
    right_slots = column_blocks.shape[2] // block_size
    target_slots = targets.shape[1]
    offsets = (jnp.arange(tile_count, dtype=jnp.int32) * tile_rows)[:, None, None]
    global_rows = (offsets + left_cols).astype(jnp.int32)
    picked = jnp.take(column_blocks, global_rows, axis=0)
    picked_cols = jnp.take(column_cols, global_rows, axis=0)
    split_right = picked.reshape(
        tile_count, row_count, left_slots, block_size, right_slots, block_size
    )
    matching = (picked_cols[:, :, :, None, :] == targets[None, :, None, :, None]).astype(
        jnp.bfloat16
    )
    chosen = jnp.einsum(
        "jgptq,jgpzqy->jgpzty", matching, split_right, preferred_element_type=jnp.float32
    ).astype(jnp.bfloat16)
    split_left = left_blocks.reshape(tile_count, row_count, block_size, left_slots, block_size)
    combined = jnp.einsum(
        "jgxpz,jgpzty->gxty", split_left, chosen, preferred_element_type=jnp.float32
    )
    return combined.reshape(row_count, block_size, target_slots * block_size)


def carry_over(second_power, square_pattern, cube_pattern):
    tile_count, row_count, block_size, width = second_power.shape
    slot_count = width // block_size
    matching = (square_pattern[:, :, None, :] == cube_pattern[:, :, :, None]).astype(jnp.float32)
    split_two = second_power.astype(jnp.float32).reshape(
        tile_count, row_count, block_size, slot_count, block_size
    )
    carried = jnp.einsum("jgtu,jgxuy->jgxty", matching, split_two, precision=lax.Precision.HIGHEST)
    return carried.reshape(tile_count, row_count, block_size, cube_pattern.shape[2] * block_size)


def on_device(density_blocks, density_columns, square_pattern, cube_pattern):
    column_blocks, column_cols = (
        lax.all_gather(density_blocks[0], ("col", "rep"), axis=0, tiled=True),
        lax.all_gather(density_columns[0], ("col", "rep"), axis=0, tiled=True),
    )
    row_blocks, row_cols = (
        lax.all_gather(density_blocks, "row", axis=0, tiled=True),
        lax.all_gather(density_columns, "row", axis=0, tiled=True),
    )
    second_power = rows_times_column(
        row_blocks, row_cols, column_blocks, column_cols, square_pattern[0]
    ).astype(jnp.bfloat16)
    square_blocks, square_cols = (
        lax.all_gather(second_power[None], "row", axis=0, tiled=True),
        lax.all_gather(square_pattern, "row", axis=0, tiled=True),
    )
    third_power = rows_times_column(
        square_blocks, square_cols, column_blocks, column_cols, cube_pattern[0]
    )
    carried = carry_over(second_power[None], square_pattern, cube_pattern)
    return 3.0 * carried - 2.0 * third_power[None]


def solution(mesh):
    return jax.shard_map(
        on_device,
        mesh=mesh,
        in_specs=(
            P("row", ("col", "rep"), None, None),
            P("row", ("col", "rep"), None),
            P("row", ("col", "rep"), None),
            P("row", ("col", "rep"), None),
        ),
        out_specs=P("row", ("col", "rep"), None, None),
        check_vma=False,
    )
```

profile of v0, /device:TPU:0, one launch (start us, length us, event | category | flops | bytes accessed | tf_op | source)
XLA Modules:
  0.0 94.1 jit_solution(12482433770231604186)
XLA Ops:
  6.5 0.0 all-gather.4.cloned.1.call-start
  6.5 0.7 all-gather.4.cloned.1.call-update
  7.3 12.8 %all_gather.19 = s32[4,2,2]{2,1,0:T(2,128)S(1)} all-gather(s32[1,2,2]{2,1,0:T(2,128)} %param.9), channel_id=1, replica_groups=mesh['row'=4,'col'=4,'rep'=2] {'row'}, dimensions={0}, use_global_device_ids=true | all-gather | bytes 80 | tf_op jit(solution)/shard_map/all_gather | solution.py:51
  20.1 7.9 %all_gather.23 = s32[4,2,2]{2,1,0:T(2,128)S(1)} all-gather(s32[1,2,2]{2,1,0:T(2,128)} %param.10), channel_id=1, replica_groups=mesh['row'=4,'col'=4,'rep'=2] {'row'}, dimensions={0}, use_global_device_ids=true | all-gather | bytes 80 | tf_op jit(solution)/shard_map/all_gather | solution.py:58
  28.0 12.9 %all-gather.1 = s32[1,16,2]{2,0,1:T(1,128)S(1)} all-gather(s32[1,2,2]{2,0,1:T(1,128)} %bitcast.78), channel_id=3, replica_groups=mesh['row'=4,'col'=4,'rep'=2] {'col','rep'}, dimensions={1}, use_global_device_ids=true | all-gather | bytes 144 | tf_op jit(solution)/shard_map/all_gather | solution.py:47
  40.9 0.1 compare_and_fusion
  41.0 0.1 reshape.136
  41.1 0.1 reshape.144
  41.2 0.1 copy.45
  41.2 0.1 copy.46
  41.3 0.6 gather_fusion.3
  41.9 0.1 copy.70
  42.0 0.6 gather_fusion.1
  42.6 0.1 copy.71
  42.8 0.1 copy.48
  42.9 16.2 %all_gather.21 = bf16[4,2,128,256]{3,2,1,0:T(8,128)(2,1)S(1)} all-gather(bf16[1,2,128,256]{3,2,1,0:T(8,128)(2,1)} %param.8), channel_id=1, replica_groups=mesh['row'=4,'col'=4,'rep'=2] {'row'}, dimensions={0}, use_global_device_ids=true | all-gather | bytes 655360 | tf_op jit(solution)/shard_map/all_gather | solution.py:50
  59.0 1.0 %copy.78 = bf16[4,2,128,256]{2,3,0,1:T(8,128)(2,1)} copy(bf16[4,2,128,256]{3,2,1,0:T(8,128)(2,1)S(1)} %all_gather.21) | data formatting | bytes 1048576 | tf_op jit(solution)/shard_map/reshape | solution.py:26
  60.1 0.1 copy.57
  60.2 0.0 all-gather.4.cloned.1.call-done
  60.2 0.0 copy-start
  60.2 1.9 %gather_fusion = bf16[16,128,256]{2,1,0:T(8,128)(2,1)S(1)} fusion(bf16[16,128,256]{2,1,0:T(8,128)(2,1)} %bitcast.69, s32[1024]{0:T(1024)S(1)} %pad_clamp_fusion.1), kind=kCustom, calls=%fused_computation.clone | custom fusion | bytes 2097216 | tf_op jit(solution)/shard_map/jit(_take)/gather | solution.py:15
  62.2 0.0 copy-done
  62.2 0.6 gather_fusion.2
  62.8 1.2 %broadcast_select_fusion = (bf16[4,2,2,128,256]{4,3,2,1,0:T(8,128)(2,1)S(1)}, bf16[4,2,2,128,256]{4,3,2,1,0:T(8,128)(2,1)}) fusion(bf16[4,2,2,128,256]{4,3,2,1,0:T(8,128)(2,1)S(1)} %bitcast.68, pred[4,2,2]{2,1,0:T(4,128)(4,1)S(1)} %get-tuple-element.6, bf16[4,2,2,128,256]{4,3,2,1,0:T(8,128)(2,1)S(1)} %bitcast.67, pred[4,2,2]{2,1,0:T(4,128)(4,1)S(1)} %get-tuple-element.11), kind=kLoop, calls=%fused_computation.15 | loop fusion | flops 1048576 | bytes 4194336 | tf_op jit(solution)/shard_map/jit(_take)/select_n | solution.py:15
  64.0 0.0 copy-start.2
  64.0 1.4 %reshape.90 = bf16[4,2,2,128,2,128]{5,4,3,2,1,0:T(2,128)(2,1)S(1)} reshape(bf16[4,2,2,128,256]{4,3,2,1,0:T(8,128)(2,1)} %get-tuple-element.14) | data formatting | bytes 2097152 | tf_op jit(solution)/shard_map/reshape | solution.py:17
  65.4 0.0 copy-done.2
  65.4 0.0 copy-start.1
  65.4 1.3 %fusion = bf16[4,2,2,128,2,128]{5,4,3,2,1,0:T(2,128)(2,1)S(1)} fusion(bf16[4,2,2,128,2,128]{5,4,3,2,1,0:T(2,128)(2,1)S(1)} %reshape.90, s32[2,2]{1,0:T(2,128)S(1)} %bitcast.80, s32[4,2,2,2]{3,2,1,0:T(2,128)S(1)} %copy.48), kind=kOutput, calls=%fused_computation.6 | convolution fusion | flops 2621504 | bytes 2097296 | tf_op jit(solution)/shard_map/jgptq,jgpzqy->jgpzty/dot_general | solution.py:23
  66.7 0.0 copy-done.1
  66.7 0.5 fusion.3
  67.3 0.1 copy.53
  67.4 15.5 %all_gather.22 = bf16[4,2,128,256]{3,2,1,0:T(8,128)(2,1)S(1)} all-gather(bf16[1,2,128,256]{3,2,1,0:T(8,128)(2,1)S(1)} %copy.53), channel_id=1, replica_groups=mesh['row'=4,'col'=4,'rep'=2] {'row'}, dimensions={0}, use_global_device_ids=true | all-gather | bytes 655360 | tf_op jit(solution)/shard_map/all_gather | solution.py:57
  82.9 0.3 copy.54
  83.2 0.0 copy-start.3
  83.2 0.3 reshape.93
  83.5 0.4 copy-done.3
  83.9 1.3 %fusion.1 = bf16[4,2,2,128,2,128]{5,4,3,2,1,0:T(2,128)(2,1)S(1)} fusion(bf16[4,2,2,128,2,128]{5,4,3,2,1,0:T(2,128)(2,1)S(1)} %reshape.93, s32[2,2]{1,0:T(2,128)S(1)} %bitcast.82, s32[4,2,2,2]{3,2,1,0:T(2,128)S(1)} %copy.57), kind=kOutput, calls=%fused_computation.7 | convolution fusion | flops 2621504 | bytes 2097296 | tf_op jit(solution)/shard_map/jgptq,jgpzqy->jgpzty/dot_general | solution.py:23
  85.2 0.5 fusion.4
  85.8 0.1 copy.52
  85.9 0.4 fusion.2
  86.3 0.1 copy.74
  86.4 0.8 copy.61
  (6 shorter events, 0.1 us)
Async XLA Ops:
  6.5 53.7 %all-gather.4.cloned.1.call-start = ((), (), s32[]{:S(2)}) async-start(), calls=%async_computation | async-start | bytes 1179648 | tf_op jit(solution)/shard_map/all_gather | solution.py:46
  60.2 1.9 %copy-start = (bf16[1,16,128,256]{3,2,0,1:T(8,128)(2,1)S(1)}, bf16[1,16,128,256]{3,2,0,1:T(8,128)(2,1)}, u32[]{:S(2)}) copy-start(bf16[1,16,128,256]{3,2,0,1:T(8,128)(2,1)} %all-gather.4.cloned.1.call-done) | copy-start | bytes 3145732
  64.0 1.4 %copy-start.2 = (s32[1,2,2]{2,1,0:T(2,128)S(1)}, s32[1,2,2]{2,1,0:T(2,128)}, u32[]{:S(2)}) copy-start(s32[1,2,2]{2,1,0:T(2,128)} %param.10) | copy-start | bytes 52
  65.4 1.3 %copy-start.1 = (bf16[4,2,128,256]{2,3,0,1:T(8,128)(2,1)S(1)}, bf16[4,2,128,256]{2,3,0,1:T(8,128)(2,1)}, u32[]{:S(2)}) copy-start(bf16[4,2,128,256]{2,3,0,1:T(8,128)(2,1)} %copy.78) | copy-start | bytes 1572868
  83.2 0.7 copy-start.3
Sparse Core Ops, SparseCore 0:
  9.2 26.1 all-gather.3
where the time goes:
time: 94.4 us; the launch traced here: 94.1 us
  blocking collectives  65.3 us (69%)
  between operations  13.6 us (14%)
  local copies, waits for them, and re-layouts  9.08 us (10%)
  matrix products  4.01 us (4%)
  other arithmetic  1.38 us (1%)
    all_gather x1, blocking collectives, on_device(): lax.all_gather(density_blocks, 'row', axis=0, tiled=True)  16.2 us
    all_gather x1, blocking collectives, on_device(): lax.all_gather(second_power[None], 'row', axis=0, tiled=True)  15.5 us
    all_gather x1, blocking collectives, on_device(): lax.all_gather(density_columns[0], ('col', 'rep'), axis=0, tiled=True)  12.9 us
    all_gather x1, blocking collectives, on_device(): lax.all_gather(density_columns, 'row', axis=0, tiled=True)  12.8 us
    all_gather x1, blocking collectives, on_device(): lax.all_gather(square_pattern, 'row', axis=0, tiled=True)  7.87 us
    dot_general x2, matrix products, rows_times_column(): jnp.einsum('jgptq,jgpzqy->jgpzty', matching, split_right, preferred_eleme...  2.6 us
    gather x2, local copies, waits for them, and re-layouts, rows_times_column(): picked = jnp.take(column_blocks, global_rows, axis=0)  2.54 us
  transfers between devices with their start and end apart: 1, of which 0 were waited for; matrix products, arithmetic and copies ran while one was open for 3% of the time, Pallas kernels for 0%

commit v1 on v0

v1 whole, which is shorter than its diff:
```python
import functools

import jax
import jax.numpy as jnp
from jax import lax
from jax.experimental import pallas as pl
from jax.experimental.pallas import tpu as pltpu
from jax.sharding import PartitionSpec as P

MESH = pl.DeviceIdType.MESH
LANES = 128


def kernel(
    sizes, idx_ref, x_ref, out_ref, row_x, row_x2, col_x, chosen, second, idx_vmem_row, idx_vmem_col,
    idx_row, idx_col, row_send, row_recv, x2_send, x2_recv, col_send, col_recv, fwd_send, fwd_recv,
    irow_send, irow_recv, icol_send, icol_recv, local_sem,
):
    n_row, n_col, n_rep, rows, size, slots, q_slots, tile_rows = sizes
    n_chip = n_col // 2
    n_plane = n_col * n_rep
    r, c, p = lax.axis_index("row"), lax.axis_index("col"), lax.axis_index("rep")
    chip, core = c // 2, c % 2
    mine = c * n_rep + p

    def place(k):
        return pl.ds(k * rows, rows)

    own_row = pltpu.make_async_copy(x_ref, row_x.at[r], local_sem.at[0])
    own_row.start()
    own_col = pltpu.make_async_copy(x_ref, col_x.at[place(mine)], local_sem.at[1])
    own_col.start()
    own_irow = pltpu.make_async_copy(idx_ref, idx_vmem_row.at[r], local_sem.at[2])
    own_irow.start()
    own_icol = pltpu.make_async_copy(idx_ref, idx_vmem_col.at[mine], local_sem.at[3])
    own_icol.start()

    row_peers = [(lax.rem(r + d, n_row), lax.rem(r + n_row - d, n_row)) for d in range(1, n_row)]
    plane_peers = []
    for dc in range(n_col):
        for dp in range(n_rep):
            if dc or dp:
                to = (lax.rem(c + dc, n_col), lax.rem(p + dp, n_rep))
                source = lax.rem(c + n_col - dc, n_col) * n_rep + lax.rem(p + n_rep - dp, n_rep)
                plane_peers.append((to, source))
    same_core = []
    for dc in range(n_chip):
        for dp in range(n_rep):
            to = (lax.rem(chip + dc, n_chip) * 2 + core, lax.rem(p + dp, n_rep))
            from_chip = lax.rem(chip + n_chip - dc, n_chip) * 2
            from_rep = lax.rem(p + n_rep - dp, n_rep)
            same_core.append(
                (to, (from_chip + core) * n_rep + from_rep, (from_chip + 1 - core) * n_rep + from_rep)
            )

    barrier = pltpu.get_barrier_semaphore()
    for to, _ in row_peers:
        pl.semaphore_signal(barrier, inc=1, device_id={"row": to}, device_id_type=MESH)
    for (to_c, to_p), _ in plane_peers:
        pl.semaphore_signal(barrier, inc=1, device_id={"col": to_c, "rep": to_p}, device_id_type=MESH)
    pl.semaphore_wait(barrier, len(row_peers) + len(plane_peers))

    def remote(src, dst, send, recv, where):
        return pltpu.make_async_remote_copy(
            src_ref=src, dst_ref=dst, send_sem=send, recv_sem=recv, device_id=where, device_id_type=MESH
        )

    sends = []

    def go(copy):
        copy.start()
        sends.append(copy)

    for i, (to, _) in enumerate(row_peers):
        go(remote(idx_ref, idx_vmem_row.at[r], irow_send.at[i], irow_recv.at[i], {"row": to}))
    for i, ((to_c, to_p), _) in enumerate(plane_peers):
        go(remote(idx_ref, idx_vmem_col.at[mine], icol_send.at[i], icol_recv.at[i], {"col": to_c, "rep": to_p}))
    for i, (to, _) in enumerate(row_peers):
        go(remote(x_ref, row_x.at[r], row_send.at[i], row_recv.at[i], {"row": to}))
    for i, ((to_c, to_p), _, _) in enumerate(same_core):
        if i:
            go(remote(x_ref, col_x.at[place(mine)], col_send.at[i], col_recv.at[i], {"col": to_c, "rep": to_p}))
    sibling = chip * 2 + 1 - core
    go(remote(x_ref, col_x.at[place(mine)], fwd_send.at[0], fwd_recv.at[0], {"col": sibling}))

    own_irow.wait()
    own_icol.wait()
    for i, (to, source) in enumerate(row_peers):
        remote(idx_ref, idx_vmem_row.at[source], irow_send.at[i], irow_recv.at[i], {"row": to}).wait_recv()
    for i, ((to_c, to_p), source) in enumerate(plane_peers):
        remote(
            idx_ref, idx_vmem_col.at[source], icol_send.at[i], icol_recv.at[i], {"col": to_c, "rep": to_p}
        ).wait_recv()
    to_smem_row = pltpu.make_async_copy(idx_vmem_row, idx_row, local_sem.at[4])
    to_smem_row.start()
    to_smem_col = pltpu.make_async_copy(idx_vmem_col, idx_col, local_sem.at[5])
    to_smem_col.start()
    to_smem_row.wait()
    to_smem_col.wait()

    for i, ((to_c, to_p), source, _) in enumerate(same_core):
        if i:
            slab = col_x.at[place(source)]
            remote(x_ref, slab, col_send.at[i], col_recv.at[i], {"col": to_c, "rep": to_p}).wait_recv()
            go(remote(slab, slab, fwd_send.at[i], fwd_recv.at[i], {"col": sibling}))
    own_col.wait()
    for i, (_, _, source) in enumerate(same_core):
        slab = col_x.at[place(source)]
        remote(slab, slab, fwd_send.at[i], fwd_recv.at[i], {"col": sibling}).wait_recv()

    square_at = rows * slots
    cube_at = square_at + rows * q_slots

    def choose(g, j, left_at, left_slots, target_at):
        none = jnp.zeros((size, size), col_x.dtype)
        for t in range(q_slots):
            s = idx_row[r, 0, target_at + g * q_slots + t]
            found = []
            for b in range(tile_rows):
                h = j * tile_rows + b
                block = none
                for q in range(slots):
                    hit = idx_col[h // rows, 0, (h % rows) * slots + q] == s
                    block = lax.select(hit, col_x[h, :, q * size:(q + 1) * size], block)
                found.append(block)
            for u in range(left_slots):
                row = idx_row[j, 0, left_at + g * left_slots + u]
                pick = none
                for b in range(tile_rows):
                    pick = lax.select(row == b, found[b], pick)
                chosen[j, g, u * size:(u + 1) * size, t * size:(t + 1) * size] = pick

    def times(left, j, g, depth):
        return jnp.dot(left, chosen[j, g, :depth], preferred_element_type=jnp.float32)

    for g in range(rows):
        for j in range(n_row):
            choose(g, j, 0, slots, square_at)
    own_row.wait()
    totals = [times(row_x[r, g], r, g, slots * size) for g in range(rows)]
    for i, (to, source) in enumerate(row_peers):
        remote(x_ref, row_x.at[source], row_send.at[i], row_recv.at[i], {"row": to}).wait_recv()
        if i < len(row_peers) - 1:
            for g in range(rows):
                totals[g] += times(row_x[source, g], source, g, slots * size)
    last = row_peers[-1][1]
    for g in range(rows):
        second[g] = (totals[g] + times(row_x[last, g], last, g, slots * size)).astype(second.dtype)
        for i, (to, _) in enumerate(row_peers):
            go(remote(second.at[g], row_x2.at[r, g], x2_send.at[i, g], x2_recv.at[i, g], {"row": to}))

    for g in range(rows):
        for j in range(n_row):
            choose(g, j, square_at, q_slots, cube_at)
    for g in range(rows):
        for t in range(q_slots):
            carried = jnp.zeros((size, size), jnp.float32)
            target = idx_row[r, 0, cube_at + g * q_slots + t]
            for u in range(q_slots):
                weight = jnp.where(idx_row[r, 0, square_at + g * q_slots + u] == target, 3.0, 0.0)
                carried += weight * second[g, :, u * size:(u + 1) * size].astype(jnp.float32)
            out_ref[0, g, :, t * size:(t + 1) * size] = carried
    for g in range(rows):
        total = times(second[g], r, g, q_slots * size)
        for i, (to, source) in enumerate(row_peers):
            remote(
                second.at[g], row_x2.at[source, g], x2_send.at[i, g], x2_recv.at[i, g], {"row": to}
            ).wait_recv()
            total += times(row_x2[source, g], source, g, q_slots * size)
        out_ref[0, g] += -2.0 * total
    for copy in sends:
        copy.wait_send()


def solution(mesh):
    n_row, n_col, n_rep = (mesh.shape[a] for a in ("row", "col", "rep"))

    def on_device(blocks, columns, square_pattern, cube_pattern):
        _, rows, size, width = blocks.shape
        slots, q_slots = columns.shape[2], square_pattern.shape[2]
        n_plane = n_col * n_rep
        n_blocks = n_plane * rows
        tile_rows = n_blocks // n_row
        flat = jnp.concatenate([a.reshape(1, -1) for a in (columns, square_pattern, cube_pattern)], axis=1)
        idx = jnp.pad(flat, ((0, 0), (0, LANES - flat.shape[1])))
        dma = pltpu.SemaphoreType.DMA
        n_same = n_plane // 2
        depth = max(slots, q_slots) * size
        return pl.pallas_call(
            functools.partial(kernel, (n_row, n_col, n_rep, rows, size, slots, q_slots, tile_rows)),
            out_shape=jax.ShapeDtypeStruct((1, rows, size, q_slots * size), jnp.float32),
            in_specs=[pl.BlockSpec(memory_space=pltpu.VMEM), pl.BlockSpec(memory_space=pl.ANY)],
            out_specs=pl.BlockSpec(memory_space=pltpu.VMEM),
            scratch_shapes=[
                pltpu.VMEM((n_row, rows, size, width), blocks.dtype),
                pltpu.VMEM((n_row, rows, size, q_slots * size), blocks.dtype),
                pltpu.VMEM((n_blocks, size, width), blocks.dtype),
                pltpu.VMEM((n_row, rows, depth, q_slots * size), blocks.dtype),
                pltpu.VMEM((rows, size, q_slots * size), blocks.dtype),
                pltpu.VMEM((n_row, 1, LANES), jnp.int32),
                pltpu.VMEM((n_plane, 1, LANES), jnp.int32),
                pltpu.SMEM((n_row, 1, LANES), jnp.int32),
                pltpu.SMEM((n_plane, 1, LANES), jnp.int32),
                dma((n_row,)), dma((n_row,)),
                dma((n_row, rows)), dma((n_row, rows)),
                dma((n_same,)), dma((n_same,)),
                dma((n_same,)), dma((n_same,)),
                dma((n_row,)), dma((n_row,)),
                dma((n_plane,)), dma((n_plane,)),
                dma((6,)),
            ],
            compiler_params=pltpu.CompilerParams(
                collective_id=0, has_side_effects=True, vmem_limit_bytes=40 * 2**20
            ),
        )(idx, blocks[0])

    return jax.shard_map(
        on_device,
        mesh=mesh,
        in_specs=(
            P("row", ("col", "rep"), None, None),
            P("row", ("col", "rep"), None),
            P("row", ("col", "rep"), None),
            P("row", ("col", "rep"), None),
        ),
        out_specs=P("row", ("col", "rep"), None, None),
        check_vma=False,
    )
```

time: 94.4 us -> 34.5 us (0.37)
  blocking collectives: 65.3 us -> 0 us
  Pallas kernels: 0 us -> 30.5 us
  between operations: 13.6 us -> 0.02 us
  local copies, waits for them, and re-layouts: 9.08 us -> 3.73 us
  matrix products: 4.01 us -> 0 us
  other arithmetic: 1.38 us -> 0.08 us
    all_gather x5 -> x0, blocking collectives: 65.3 us -> none  [the longest x1 16.2 us: on_device(): lax.all_gather(density_blocks, 'row', axis=0, tiled=True)]
    pallas_call x0 -> x1, Pallas kernels: none -> 30.5 us  [on_device(): pl.pallas_call(functools.partial(kernel, (n_row, n_col, n_rep, rows, size...]
    dot_general x5 -> x0, matrix products: 4.01 us -> none  [the longest x2 2.6 us: rows_times_column(): jnp.einsum('jgptq,jgpzqy->jgpzty', matching, split_right, preferred_eleme...]
    gather x6 -> x0, local copies, waits for them, and re-layouts: 3.94 us -> none  [the longest x2 2.54 us: rows_times_column(): picked = jnp.take(column_blocks, global_rows, axis=0)]
    unnamed x8 -> x9, local copies, waits for them, and re-layouts: 0.39 us -> 3.48 us
    reshape x3, local copies, waits for them, and re-layouts: 2.67 us -> 0.24 us  [on_device(): a.reshape(1, -1)]
    select_n x2 -> x0, other arithmetic: 1.23 us -> none  [the longest x1 1.22 us: rows_times_column(): picked = jnp.take(column_blocks, global_rows, axis=0)]
  transfers between devices with their start and end apart: 1 -> 0, of which waited for: 0 -> 0; matrix products, arithmetic and copies ran while one was open for 3% -> 0% of each run, Pallas kernels for 0% -> 0%
where the time goes in v1:
time: 34.5 us; the launch traced here: 34.3 us
  Pallas kernels  30.5 us (88%)
  local copies, waits for them, and re-layouts  3.73 us (11%)
    pallas_call x1, Pallas kernels, on_device(): pl.pallas_call(functools.partial(kernel, (n_row, n_col, n_rep, rows, size...  30.5 us
    unnamed x9, local copies, waits for them, and re-layouts  3.48 us

profile of v1, /device:TPU:0, one launch (start us, length us, event | category | flops | bytes accessed | tf_op | source)
XLA Modules:
  0.0 34.3 jit_solution(11020160259285539768)
XLA Ops:
  0.0 0.0 copy-start.1
  0.0 0.7 %copy-done.1 = s32[1,2,2]{2,1,0:T(2,128)S(1)} copy-done((s32[1,2,2]{2,1,0:T(2,128)S(1)}, s32[1,2,2]{2,1,0:T(2,128)}, u32[]{:S(2)}) %copy-start.1) | copy-done | bytes 40
  0.7 0.0 copy-start.2
  0.7 0.1 reshape.9
  0.8 0.6 %copy-done.2 = s32[1,2,2]{2,1,0:T(2,128)S(1)} copy-done((s32[1,2,2]{2,1,0:T(2,128)S(1)}, s32[1,2,2]{2,1,0:T(2,128)}, u32[]{:S(2)}) %copy-start.2) | copy-done | bytes 40
  1.4 0.0 copy-start.3
  1.4 0.1 reshape.10
  1.4 0.6 %copy-done.3 = s32[1,2,2]{2,1,0:T(2,128)S(1)} copy-done((s32[1,2,2]{2,1,0:T(2,128)S(1)}, s32[1,2,2]{2,1,0:T(2,128)}, u32[]{:S(2)}) %copy-start.3) | copy-done | bytes 40
  2.0 0.1 reshape.11
  2.1 0.1 pad_add_fusion
  2.2 0.0 copy-start
  2.2 0.9 %copy-done = bf16[1,2,128,256]{3,2,1,0:T(8,128)(2,1)S(1)} copy-done((bf16[1,2,128,256]{3,2,1,0:T(8,128)(2,1)S(1)}, bf16[1,2,128,256]{3,2,1,0:T(8,128)(2,1)}, u32[]{:S(2)}) %copy-start) | copy-done | bytes 131096
  3.1 30.5 %shard_map.46 = f32[1,2,128,256]{3,2,1,0:T(8,128)S(1)} custom-call(s32[1,128]{1,0:T(1,128)S(1)} %pad.4.idx_ref, bf16[2,128,256]{2,1,0:T(8,128)(2,1)S(1)} %bitcast.1), custom_call_target="tpu_custom_call" | custom-call | tf_op jit(solution)/shard_map/pallas_call | solution.py:189
  33.6 0.7 %copy.6 = f32[1,2,128,256]{3,2,1,0:T(8,128)} copy(f32[1,2,128,256]{3,2,1,0:T(8,128)S(1)} %shard_map.46) | data formatting | bytes 524288
  (1 shorter events, 0.0 us)
Async XLA Ops:
  0.0 0.7 %copy-start.1 = (s32[1,2,2]{2,1,0:T(2,128)S(1)}, s32[1,2,2]{2,1,0:T(2,128)}, u32[]{:S(2)}) copy-start(s32[1,2,2]{2,1,0:T(2,128)} %param.5) | copy-start | bytes 52
  0.7 0.7 %copy-start.2 = (s32[1,2,2]{2,1,0:T(2,128)S(1)}, s32[1,2,2]{2,1,0:T(2,128)}, u32[]{:S(2)}) copy-start(s32[1,2,2]{2,1,0:T(2,128)} %param.6) | copy-start | bytes 52
  1.4 0.7 %copy-start.3 = (s32[1,2,2]{2,1,0:T(2,128)S(1)}, s32[1,2,2]{2,1,0:T(2,128)}, u32[]{:S(2)}) copy-start(s32[1,2,2]{2,1,0:T(2,128)} %param.7) | copy-start | bytes 52
  2.2 0.9 %copy-start = (bf16[1,2,128,256]{3,2,1,0:T(8,128)(2,1)S(1)}, bf16[1,2,128,256]{3,2,1,0:T(8,128)(2,1)}, u32[]{:S(2)}) copy-start(bf16[1,2,128,256]{3,2,1,0:T(8,128)(2,1)} %param.4) | copy-start | bytes 393220

commit v2 on v1

v2 whole, which is shorter than its diff:
```python
import functools

import jax
import jax.numpy as jnp
from jax import lax
from jax.experimental import pallas as pl
from jax.experimental.pallas import tpu as pltpu
from jax.sharding import PartitionSpec as P

MESH = pl.DeviceIdType.MESH


def kernel(
    sizes, dc_ref, sq_ref, cu_ref, x_ref, out_ref, row_x, row_x2, col_x, chosen, second, dc_row_v, sq_row_v, dc_col_v,
    dc_row, sq_row, dc_col, cube, row_send, row_recv, x2_send, x2_recv, col_send, col_recv, fwd_send, fwd_recv,
    irow_send, irow_recv, icol_send, icol_recv, local_sem,
):
    n_row, n_col, n_rep, rows, size, slots, q_slots, tile_rows = sizes
    n_chip = n_col // 2
    n_plane = n_col * n_rep
    r, c, p = lax.axis_index("row"), lax.axis_index("col"), lax.axis_index("rep")
    chip, core = c // 2, c % 2
    mine = c * n_rep + p

    def place(k):
        return pl.ds(k * rows, rows)

    own_row = pltpu.make_async_copy(x_ref, row_x.at[r], local_sem.at[0])
    own_row.start()
    own_col = pltpu.make_async_copy(x_ref, col_x.at[place(mine)], local_sem.at[1])
    own_col.start()
    own_ints = [
        pltpu.make_async_copy(dc_ref, dc_row_v.at[r], local_sem.at[2]),
        pltpu.make_async_copy(sq_ref, sq_row_v.at[r], local_sem.at[3]),
        pltpu.make_async_copy(dc_ref, dc_col_v.at[mine], local_sem.at[4]),
    ]
    own_cube = pltpu.make_async_copy(cu_ref, cube, local_sem.at[5])
    for copy in (*own_ints, own_cube):
        copy.start()

    row_peers = [(lax.rem(r + d, n_row), lax.rem(r + n_row - d, n_row)) for d in range(1, n_row)]
    plane_peers = []
    for dc in range(n_col):
        for dp in range(n_rep):
            if dc or dp:
                to = (lax.rem(c + dc, n_col), lax.rem(p + dp, n_rep))
                source = lax.rem(c + n_col - dc, n_col) * n_rep + lax.rem(p + n_rep - dp, n_rep)
                plane_peers.append((to, source))
    same_core = []
    for dc in range(n_chip):
        for dp in range(n_rep):
            to = (lax.rem(chip + dc, n_chip) * 2 + core, lax.rem(p + dp, n_rep))
            from_chip = lax.rem(chip + n_chip - dc, n_chip) * 2
            from_rep = lax.rem(p + n_rep - dp, n_rep)
            same_core.append(
                (to, (from_chip + core) * n_rep + from_rep, (from_chip + 1 - core) * n_rep + from_rep)
            )

    barrier = pltpu.get_barrier_semaphore()
    for to, _ in row_peers:
        pl.semaphore_signal(barrier, inc=1, device_id={"row": to}, device_id_type=MESH)
    for (to_c, to_p), _ in plane_peers:
        pl.semaphore_signal(barrier, inc=1, device_id={"col": to_c, "rep": to_p}, device_id_type=MESH)
    pl.semaphore_wait(barrier, len(row_peers) + len(plane_peers))

    def remote(src, dst, send, recv, where):
        return pltpu.make_async_remote_copy(
            src_ref=src, dst_ref=dst, send_sem=send, recv_sem=recv, device_id=where, device_id_type=MESH
        )

    sends = []

    def go(copy):
        copy.start()
        sends.append(copy)

    for i, ((to_c, to_p), _) in enumerate(plane_peers):
        go(remote(dc_ref, dc_col_v.at[mine], icol_send.at[i], icol_recv.at[i], {"col": to_c, "rep": to_p}))
    for i, (to, _) in enumerate(row_peers):
        go(remote(dc_ref, dc_row_v.at[r], irow_send.at[i, 0], irow_recv.at[i, 0], {"row": to}))
        go(remote(sq_ref, sq_row_v.at[r], irow_send.at[i, 1], irow_recv.at[i, 1], {"row": to}))
    for i, (to, _) in enumerate(row_peers):
        go(remote(x_ref.at[0], row_x.at[r, 0], row_send.at[i, 0], row_recv.at[i, 0], {"row": to}))
    sibling = chip * 2 + 1 - core
    for i, ((to_c, to_p), _, _) in enumerate(same_core):
        if i:
            go(remote(x_ref, col_x.at[place(mine)], col_send.at[i], col_recv.at[i], {"col": to_c, "rep": to_p}))
    go(remote(x_ref, col_x.at[place(mine)], fwd_send.at[0], fwd_recv.at[0], {"col": sibling}))
    for g in range(1, rows):
        for i, (to, _) in enumerate(row_peers):
            go(remote(x_ref.at[g], row_x.at[r, g], row_send.at[i, g], row_recv.at[i, g], {"row": to}))

    for copy in own_ints:
        copy.wait()
    for i, ((to_c, to_p), source) in enumerate(plane_peers):
        remote(
            dc_ref, dc_col_v.at[source], icol_send.at[i], icol_recv.at[i], {"col": to_c, "rep": to_p}
        ).wait_recv()
    for i, (to, source) in enumerate(row_peers):
        remote(dc_ref, dc_row_v.at[source], irow_send.at[i, 0], irow_recv.at[i, 0], {"row": to}).wait_recv()
        remote(sq_ref, sq_row_v.at[source], irow_send.at[i, 1], irow_recv.at[i, 1], {"row": to}).wait_recv()
    to_smem = [
        pltpu.make_async_copy(dc_row_v, dc_row, local_sem.at[2]),
        pltpu.make_async_copy(sq_row_v, sq_row, local_sem.at[3]),
        pltpu.make_async_copy(dc_col_v, dc_col, local_sem.at[4]),
    ]
    for copy in to_smem:
        copy.start()

    for i, ((to_c, to_p), source, _) in enumerate(same_core):
        if i:
            slab = col_x.at[place(source)]
            remote(x_ref, slab, col_send.at[i], col_recv.at[i], {"col": to_c, "rep": to_p}).wait_recv()
            go(remote(slab, slab, fwd_send.at[i], fwd_recv.at[i], {"col": sibling}))
    own_col.wait()
    for i, (_, _, source) in enumerate(same_core):
        slab = col_x.at[place(source)]
        remote(slab, slab, fwd_send.at[i], fwd_recv.at[i], {"col": sibling}).wait_recv()

    for copy in to_smem:
        copy.wait()
    own_cube.wait()

    def choose(g, j, left, left_slots, target):
        none = jnp.zeros((size, size), col_x.dtype)
        for t in range(q_slots):
            s = target(g, t)
            found = []
            for b in range(tile_rows):
                h = j * tile_rows + b
                block = none
                for q in range(slots):
                    hit = dc_col[h // rows, h % rows, q] == s
                    block = lax.select(hit, col_x[h, :, q * size:(q + 1) * size], block)
                found.append(block)
            for u in range(left_slots):
                row = left[j, g, u]
                pick = none
                for b in range(tile_rows):
                    pick = lax.select(row == b, found[b], pick)
                chosen[j, g, u * size:(u + 1) * size, t * size:(t + 1) * size] = pick

    def times(left, j, g, depth):
        return jnp.dot(left, chosen[j, g, :depth], preferred_element_type=jnp.float32)

    def square_target(g, t):
        return sq_row[r, g, t]

    def cube_target(g, t):
        return cube[g, t]

    for g in range(rows):
        for j in range(n_row):
            choose(g, j, dc_row, slots, square_target)
    own_row.wait()
    for g in range(rows):
        total = times(row_x[r, g], r, g, slots * size)
        for i, (to, source) in enumerate(row_peers):
            remote(x_ref.at[g], row_x.at[source, g], row_send.at[i, g], row_recv.at[i, g], {"row": to}).wait_recv()
            total += times(row_x[source, g], source, g, slots * size)
        second[g] = total.astype(second.dtype)
        for i, (to, _) in enumerate(row_peers):
            go(remote(second.at[g], row_x2.at[r, g], x2_send.at[i, g], x2_recv.at[i, g], {"row": to}))
        for j in range(n_row):
            choose(g, j, sq_row, q_slots, cube_target)
        for t in range(q_slots):
            carried = jnp.zeros((size, size), jnp.float32)
            for u in range(q_slots):
                weight = jnp.where(sq_row[r, g, u] == cube[g, t], 3.0, 0.0)
                carried += weight * second[g, :, u * size:(u + 1) * size].astype(jnp.float32)
            out_ref[0, g, :, t * size:(t + 1) * size] = carried
    for g in range(rows):
        total = times(second[g], r, g, q_slots * size)
        for i, (to, source) in enumerate(row_peers):
            remote(
                second.at[g], row_x2.at[source, g], x2_send.at[i, g], x2_recv.at[i, g], {"row": to}
            ).wait_recv()
            total += times(row_x2[source, g], source, g, q_slots * size)
        out_ref[0, g] += -2.0 * total
    for copy in sends:
        copy.wait_send()


def solution(mesh):
    n_row, n_col, n_rep = (mesh.shape[a] for a in ("row", "col", "rep"))

    def on_device(blocks, columns, square_pattern, cube_pattern):
        _, rows, size, width = blocks.shape
        slots, q_slots = columns.shape[2], square_pattern.shape[2]
        n_plane = n_col * n_rep
        n_blocks = n_plane * rows
        tile_rows = n_blocks // n_row
        dma = pltpu.SemaphoreType.DMA
        n_same = n_plane // 2
        depth = max(slots, q_slots) * size
        return pl.pallas_call(
            functools.partial(kernel, (n_row, n_col, n_rep, rows, size, slots, q_slots, tile_rows)),
            out_shape=jax.ShapeDtypeStruct((1, rows, size, q_slots * size), jnp.float32),
            in_specs=[pl.BlockSpec(memory_space=pl.ANY)] * 4,
            out_specs=pl.BlockSpec(memory_space=pltpu.VMEM),
            scratch_shapes=[
                pltpu.VMEM((n_row, rows, size, width), blocks.dtype),
                pltpu.VMEM((n_row, rows, size, q_slots * size), blocks.dtype),
                pltpu.VMEM((n_blocks, size, width), blocks.dtype),
                pltpu.VMEM((n_row, rows, depth, q_slots * size), blocks.dtype),
                pltpu.VMEM((rows, size, q_slots * size), blocks.dtype),
                pltpu.VMEM((n_row, rows, slots), jnp.int32),
                pltpu.VMEM((n_row, rows, q_slots), jnp.int32),
                pltpu.VMEM((n_plane, rows, slots), jnp.int32),
                pltpu.SMEM((n_row, rows, slots), jnp.int32),
                pltpu.SMEM((n_row, rows, q_slots), jnp.int32),
                pltpu.SMEM((n_plane, rows, slots), jnp.int32),
                pltpu.SMEM((rows, q_slots), jnp.int32),
                dma((n_row, rows)), dma((n_row, rows)),
                dma((n_row, rows)), dma((n_row, rows)),
                dma((n_same,)), dma((n_same,)),
                dma((n_same,)), dma((n_same,)),
                dma((n_row, 2)), dma((n_row, 2)),
                dma((n_plane,)), dma((n_plane,)),
                dma((6,)),
            ],
            compiler_params=pltpu.CompilerParams(
                collective_id=0, has_side_effects=True, vmem_limit_bytes=60 * 2**20
            ),
        )(columns[0], square_pattern[0], cube_pattern[0], blocks[0])

    return jax.shard_map(
        on_device,
        mesh=mesh,
        in_specs=(
            P("row", ("col", "rep"), None, None),
            P("row", ("col", "rep"), None),
            P("row", ("col", "rep"), None),
            P("row", ("col", "rep"), None),
        ),
        out_specs=P("row", ("col", "rep"), None, None),
        check_vma=False,
    )
```

time: 34.5 us -> 33.3 us (0.965)
  local copies, waits for them, and re-layouts: 3.73 us -> 1.67 us
  Pallas kernels: 30.5 us -> 31.5 us
    unnamed x9 -> x1, local copies, waits for them, and re-layouts: 3.48 us -> 1.67 us
    pallas_call x1, Pallas kernels: 30.5 us -> 31.5 us  [on_device(): pl.pallas_call(functools.partial(kernel, (n_row, n_col, n_rep, rows, size...]
where the time goes in v2:
time: 33.3 us; the launch traced here: 33.1 us
  Pallas kernels  31.5 us (95%)
  local copies, waits for them, and re-layouts  1.67 us (5%)
    pallas_call x1, Pallas kernels, on_device(): pl.pallas_call(functools.partial(kernel, (n_row, n_col, n_rep, rows, size...  31.5 us
    unnamed x1, local copies, waits for them, and re-layouts  1.67 us

profile of v2, /device:TPU:0, one launch (start us, length us, event | category | flops | bytes accessed | tf_op | source)
XLA Modules:
  0.0 33.1 jit_solution(14782663821907393269)
XLA Ops:
  0.0 31.5 %shard_map.46 = f32[1,2,128,256]{3,2,1,0:T(8,128)} custom-call(s32[2,2]{1,0:T(2,128)} %bitcast.5, s32[2,2]{1,0:T(2,128)} %bitcast.6, s32[2,2]{1,0:T(2,128)} %bitcast.7, bf16[2,128,256]{2,1,0:T(8,128)(2,1)} %bitcast.4), custom_call_target="tpu_custom_call" | custom-call | tf_op jit(solution)/shard_map/pallas_call | solution.py:196
  31.5 1.7 %copy.6 = f32[1,2,128,256]{3,2,1,0:T(8,128)} copy(f32[1,2,128,256]{3,2,1,0:T(8,128)} %shard_map.46) | data formatting | bytes 524288

commit v3 on v2

--- a/solution.py
+++ b/solution.py
@@ -90,6 +90,11 @@
         for i, (to, _) in enumerate(row_peers):
             go(remote(x_ref.at[g], row_x.at[r, g], row_send.at[i, g], row_recv.at[i, g], {"row": to}))
 
+    for i, ((to_c, to_p), source, _) in enumerate(same_core):
+        if i:
+            slab = col_x.at[place(source)]
+            remote(x_ref, slab, col_send.at[i], col_recv.at[i], {"col": to_c, "rep": to_p}).wait_recv()
+            go(remote(slab, slab, fwd_send.at[i], fwd_recv.at[i], {"col": sibling}))
     for copy in own_ints:
         copy.wait()
     for i, ((to_c, to_p), source) in enumerate(plane_peers):
@@ -107,11 +112,6 @@
     for copy in to_smem:
         copy.start()
 
-    for i, ((to_c, to_p), source, _) in enumerate(same_core):
-        if i:
-            slab = col_x.at[place(source)]
-            remote(x_ref, slab, col_send.at[i], col_recv.at[i], {"col": to_c, "rep": to_p}).wait_recv()
-            go(remote(slab, slab, fwd_send.at[i], fwd_recv.at[i], {"col": sibling}))
     own_col.wait()
     for i, (_, _, source) in enumerate(same_core):
         slab = col_x.at[place(source)]
@@ -149,11 +149,10 @@
     def cube_target(g, t):
         return cube[g, t]
 
+    own_row.wait()
     for g in range(rows):
         for j in range(n_row):
             choose(g, j, dc_row, slots, square_target)
-    own_row.wait()
-    for g in range(rows):
         total = times(row_x[r, g], r, g, slots * size)
         for i, (to, source) in enumerate(row_peers):
             remote(x_ref.at[g], row_x.at[source, g], row_send.at[i, g], row_recv.at[i, g], {"row": to}).wait_recv()
@@ -161,6 +160,7 @@
         second[g] = total.astype(second.dtype)
         for i, (to, _) in enumerate(row_peers):
             go(remote(second.at[g], row_x2.at[r, g], x2_send.at[i, g], x2_recv.at[i, g], {"row": to}))
+    for g in range(rows):
         for j in range(n_row):
             choose(g, j, sq_row, q_slots, cube_target)
         for t in range(q_slots):
@@ -196,7 +196,7 @@
         return pl.pallas_call(
             functools.partial(kernel, (n_row, n_col, n_rep, rows, size, slots, q_slots, tile_rows)),
             out_shape=jax.ShapeDtypeStruct((1, rows, size, q_slots * size), jnp.float32),
-            in_specs=[pl.BlockSpec(memory_space=pl.ANY)] * 4,
+            in_specs=[pl.BlockSpec(memory_space=pltpu.HBM)] * 4,
             out_specs=pl.BlockSpec(memory_space=pltpu.VMEM),
             scratch_shapes=[
                 pltpu.VMEM((n_row, rows, size, width), blocks.dtype),
@@ -220,7 +220,7 @@
                 dma((6,)),
             ],
             compiler_params=pltpu.CompilerParams(
-                collective_id=0, has_side_effects=True, vmem_limit_bytes=60 * 2**20
+                collective_id=0, has_side_effects=True, vmem_limit_bytes=32 * 2**20
             ),
         )(columns[0], square_pattern[0], cube_pattern[0], blocks[0])
 

time: 33.3 us -> 33.1 us (level)
  Pallas kernels: 31.5 us -> 30.7 us
  local copies, waits for them, and re-layouts: 1.67 us -> 2.32 us
    pallas_call x1, Pallas kernels: 31.5 us -> 30.7 us  [on_device(): pl.pallas_call(functools.partial(kernel, (n_row, n_col, n_rep, rows, size...]
    unnamed x1 -> x9, local copies, waits for them, and re-layouts: 1.67 us -> 2.32 us
where the time goes in v3:
time: 33.1 us; the launch traced here: 33 us
  Pallas kernels  30.7 us (93%)
  local copies, waits for them, and re-layouts  2.32 us (7%)
    pallas_call x1, Pallas kernels, on_device(): pl.pallas_call(functools.partial(kernel, (n_row, n_col, n_rep, rows, size...  30.7 us
    unnamed x9, local copies, waits for them, and re-layouts  2.32 us

profile of v3, /device:TPU:0, one launch (start us, length us, event | category | flops | bytes accessed | tf_op | source)
XLA Modules:
  0.0 33.0 jit_solution(14479338096771355003)
XLA Ops:
  0.0 0.0 copy-start.2
  0.0 0.0 copy-start.3
  0.0 0.0 copy-start.1
  0.0 0.7 %copy-done.2 = s32[1,2,2]{2,1,0:T(2,128)S(1)} copy-done((s32[1,2,2]{2,1,0:T(2,128)S(1)}, s32[1,2,2]{2,1,0:T(2,128)}, u32[]{:S(2)}) %copy-start.2) | copy-done | bytes 40
  0.7 0.0 copy-done.3
  0.7 0.0 copy-done.1
  0.7 0.0 copy-start
  0.7 0.9 %copy-done = bf16[1,2,128,256]{3,2,1,0:T(8,128)(2,1)S(1)} copy-done((bf16[1,2,128,256]{3,2,1,0:T(8,128)(2,1)S(1)}, bf16[1,2,128,256]{3,2,1,0:T(8,128)(2,1)}, u32[]{:S(2)}) %copy-start) | copy-done | bytes 131096
  1.6 30.7 %shard_map.46 = f32[1,2,128,256]{3,2,1,0:T(8,128)S(1)} custom-call(s32[2,2]{1,0:T(2,128)S(1)} %bitcast.5, s32[2,2]{1,0:T(2,128)S(1)} %bitcast.6, s32[2,2]{1,0:T(2,128)S(1)} %bitcast.7, bf16[2,128,256]{2,1,0:T(8,128)(2,1)S(1)} %bitcast.4), custom_call_target="tpu_custom_call" | custom-call | tf_op jit(solution)/shard_map/pallas_call | solution.py:196
  32.3 0.7 %copy.6 = f32[1,2,128,256]{3,2,1,0:T(8,128)} copy(f32[1,2,128,256]{3,2,1,0:T(8,128)S(1)} %shard_map.46) | data formatting | bytes 524288
Async XLA Ops:
  0.0 0.7 %copy-start.2 = (s32[1,2,2]{2,1,0:T(2,128)S(1)}, s32[1,2,2]{2,1,0:T(2,128)}, u32[]{:S(2)}) copy-start(s32[1,2,2]{2,1,0:T(2,128)} %param.6) | copy-start | bytes 52
  0.0 0.7 %copy-start.3 = (s32[1,2,2]{2,1,0:T(2,128)S(1)}, s32[1,2,2]{2,1,0:T(2,128)}, u32[]{:S(2)}) copy-start(s32[1,2,2]{2,1,0:T(2,128)} %param.7) | copy-start | bytes 52
  0.0 0.7 %copy-start.1 = (s32[1,2,2]{2,1,0:T(2,128)S(1)}, s32[1,2,2]{2,1,0:T(2,128)}, u32[]{:S(2)}) copy-start(s32[1,2,2]{2,1,0:T(2,128)} %param.5) | copy-start | bytes 52
  0.7 0.9 %copy-start = (bf16[1,2,128,256]{3,2,1,0:T(8,128)(2,1)S(1)}, bf16[1,2,128,256]{3,2,1,0:T(8,128)(2,1)}, u32[]{:S(2)}) copy-start(bf16[1,2,128,256]{3,2,1,0:T(8,128)(2,1)} %param.4) | copy-start | bytes 393220

commit v4 on v3

--- a/solution.py
+++ b/solution.py
@@ -74,18 +74,18 @@
         copy.start()
         sends.append(copy)
 
+    sibling = chip * 2 + 1 - core
+    for i, ((to_c, to_p), _, _) in enumerate(same_core):
+        if i:
+            go(remote(x_ref, col_x.at[place(mine)], col_send.at[i], col_recv.at[i], {"col": to_c, "rep": to_p}))
+    go(remote(x_ref, col_x.at[place(mine)], fwd_send.at[0], fwd_recv.at[0], {"col": sibling}))
+    for i, (to, _) in enumerate(row_peers):
+        go(remote(x_ref.at[0], row_x.at[r, 0], row_send.at[i, 0], row_recv.at[i, 0], {"row": to}))
     for i, ((to_c, to_p), _) in enumerate(plane_peers):
         go(remote(dc_ref, dc_col_v.at[mine], icol_send.at[i], icol_recv.at[i], {"col": to_c, "rep": to_p}))
     for i, (to, _) in enumerate(row_peers):
         go(remote(dc_ref, dc_row_v.at[r], irow_send.at[i, 0], irow_recv.at[i, 0], {"row": to}))
         go(remote(sq_ref, sq_row_v.at[r], irow_send.at[i, 1], irow_recv.at[i, 1], {"row": to}))
-    for i, (to, _) in enumerate(row_peers):
-        go(remote(x_ref.at[0], row_x.at[r, 0], row_send.at[i, 0], row_recv.at[i, 0], {"row": to}))
-    sibling = chip * 2 + 1 - core
-    for i, ((to_c, to_p), _, _) in enumerate(same_core):
-        if i:
-            go(remote(x_ref, col_x.at[place(mine)], col_send.at[i], col_recv.at[i], {"col": to_c, "rep": to_p}))
-    go(remote(x_ref, col_x.at[place(mine)], fwd_send.at[0], fwd_recv.at[0], {"col": sibling}))
     for g in range(1, rows):
         for i, (to, _) in enumerate(row_peers):
             go(remote(x_ref.at[g], row_x.at[r, g], row_send.at[i, g], row_recv.at[i, g], {"row": to}))

time: 33.1 us -> 33.2 us (level)
  no operation moved by 1% of the time
where the time goes in v4:
time: 33.2 us; the launch traced here: 33 us
  Pallas kernels  30.7 us (92%)
  local copies, waits for them, and re-layouts  2.32 us (7%)
    pallas_call x1, Pallas kernels, on_device(): pl.pallas_call(functools.partial(kernel, (n_row, n_col, n_rep, rows, size...  30.7 us
    unnamed x9, local copies, waits for them, and re-layouts  2.32 us

profile of v4, /device:TPU:0, one launch (start us, length us, event | category | flops | bytes accessed | tf_op | source)
XLA Modules:
  0.0 33.0 jit_solution(606855418587281586)
XLA Ops:
  0.0 0.0 copy-start.2
  0.0 0.0 copy-start.3
  0.0 0.0 copy-start.1
  0.0 0.7 %copy-done.2 = s32[1,2,2]{2,1,0:T(2,128)S(1)} copy-done((s32[1,2,2]{2,1,0:T(2,128)S(1)}, s32[1,2,2]{2,1,0:T(2,128)}, u32[]{:S(2)}) %copy-start.2) | copy-done | bytes 40
  0.7 0.0 copy-done.3
  0.7 0.0 copy-done.1
  0.7 0.0 copy-start
  0.7 0.9 %copy-done = bf16[1,2,128,256]{3,2,1,0:T(8,128)(2,1)S(1)} copy-done((bf16[1,2,128,256]{3,2,1,0:T(8,128)(2,1)S(1)}, bf16[1,2,128,256]{3,2,1,0:T(8,128)(2,1)}, u32[]{:S(2)}) %copy-start) | copy-done | bytes 131096
  1.6 30.7 %shard_map.46 = f32[1,2,128,256]{3,2,1,0:T(8,128)S(1)} custom-call(s32[2,2]{1,0:T(2,128)S(1)} %bitcast.5, s32[2,2]{1,0:T(2,128)S(1)} %bitcast.6, s32[2,2]{1,0:T(2,128)S(1)} %bitcast.7, bf16[2,128,256]{2,1,0:T(8,128)(2,1)S(1)} %bitcast.4), custom_call_target="tpu_custom_call" | custom-call | tf_op jit(solution)/shard_map/pallas_call | solution.py:196
  32.3 0.7 %copy.6 = f32[1,2,128,256]{3,2,1,0:T(8,128)} copy(f32[1,2,128,256]{3,2,1,0:T(8,128)S(1)} %shard_map.46) | data formatting | bytes 524288
Async XLA Ops:
  0.0 0.7 %copy-start.2 = (s32[1,2,2]{2,1,0:T(2,128)S(1)}, s32[1,2,2]{2,1,0:T(2,128)}, u32[]{:S(2)}) copy-start(s32[1,2,2]{2,1,0:T(2,128)} %param.6) | copy-start | bytes 52
  0.0 0.7 %copy-start.3 = (s32[1,2,2]{2,1,0:T(2,128)S(1)}, s32[1,2,2]{2,1,0:T(2,128)}, u32[]{:S(2)}) copy-start(s32[1,2,2]{2,1,0:T(2,128)} %param.7) | copy-start | bytes 52
  0.0 0.7 %copy-start.1 = (s32[1,2,2]{2,1,0:T(2,128)S(1)}, s32[1,2,2]{2,1,0:T(2,128)}, u32[]{:S(2)}) copy-start(s32[1,2,2]{2,1,0:T(2,128)} %param.5) | copy-start | bytes 52
  0.7 0.9 %copy-start = (bf16[1,2,128,256]{3,2,1,0:T(8,128)(2,1)S(1)}, bf16[1,2,128,256]{3,2,1,0:T(8,128)(2,1)}, u32[]{:S(2)}) copy-start(bf16[1,2,128,256]{3,2,1,0:T(8,128)(2,1)} %param.4) | copy-start | bytes 393220

commit v5 on v3

--- a/solution.py
+++ b/solution.py
@@ -220,7 +220,7 @@
                 dma((6,)),
             ],
             compiler_params=pltpu.CompilerParams(
-                collective_id=0, has_side_effects=True, vmem_limit_bytes=32 * 2**20
+                collective_id=0, has_side_effects=True, vmem_limit_bytes=60 * 2**20
             ),
         )(columns[0], square_pattern[0], cube_pattern[0], blocks[0])
 

time: 33.1 us -> 33.3 us (level)
  Pallas kernels: 30.7 us -> 31.5 us
  local copies, waits for them, and re-layouts: 2.32 us -> 1.67 us
    pallas_call x1, Pallas kernels: 30.7 us -> 31.5 us  [on_device(): pl.pallas_call(functools.partial(kernel, (n_row, n_col, n_rep, rows, size...]
    unnamed x9 -> x1, local copies, waits for them, and re-layouts: 2.32 us -> 1.67 us
where the time goes in v5:
time: 33.3 us; the launch traced here: 33.1 us
  Pallas kernels  31.5 us (95%)
  local copies, waits for them, and re-layouts  1.67 us (5%)
    pallas_call x1, Pallas kernels, on_device(): pl.pallas_call(functools.partial(kernel, (n_row, n_col, n_rep, rows, size...  31.5 us
    unnamed x1, local copies, waits for them, and re-layouts  1.67 us

profile of v5, /device:TPU:0, one launch (start us, length us, event | category | flops | bytes accessed | tf_op | source)
XLA Modules:
  0.0 33.1 jit_solution(1698837645971828612)
XLA Ops:
  0.0 31.5 %shard_map.46 = f32[1,2,128,256]{3,2,1,0:T(8,128)} custom-call(s32[2,2]{1,0:T(2,128)} %bitcast.5, s32[2,2]{1,0:T(2,128)} %bitcast.6, s32[2,2]{1,0:T(2,128)} %bitcast.7, bf16[2,128,256]{2,1,0:T(8,128)(2,1)} %bitcast.4), custom_call_target="tpu_custom_call" | custom-call | tf_op jit(solution)/shard_map/pallas_call | solution.py:196
  31.5 1.7 %copy.6 = f32[1,2,128,256]{3,2,1,0:T(8,128)} copy(f32[1,2,128,256]{3,2,1,0:T(8,128)} %shard_map.46) | data formatting | bytes 524288
